TPU v7x, 32 devices: a whole 2x2x4 slice. The times are simulated.
32 devices in a mesh: grp: 2 (over x), blk: 8 (over z, y), sum: 2 (over core).
Axes of the slice: x: 2, y: 2, z: 4, core: 2. Of those that a mesh axis runs over, the one named last changes fastest.
Arguments:
- points: bfloat16 [32768, 512], P(('grp', 'blk')), parts along dimension 0, may hold values from -6 to 6
- centers: bfloat16 [2048, 512], P(('blk', 'sum')), may hold values from -6 to 6
- coefficients: bfloat16 [2048, 256], P(('blk', 'sum')), may hold values from -60 to 60
- targets: float32 [32768, 256], P(('grp', 'blk'), 'sum'), parts along dimension 0, may hold values from -6 to 6
Outputs:
- residual: float32 [32768, 256], P(('grp', 'blk'), 'sum'), parts along dimension 0
There are 2 independent parts, one for each index of `grp`. A program takes and returns all parts, laid end to end along the dimension named above; an argument that names none is the same for every part. Nothing has to cross between parts.
All inputs are finite; a program needn't handle non-finite values.
Results may differ from a plain program's by a relative error of at most 0.0029.
Values may be sent and summed in bfloat16 or wider, within the bound.
A program may use at most 64 MiB of HBM per device.

v0:
```python
import math

import jax
import jax.numpy as jnp
from jax import lax
from jax.sharding import PartitionSpec as P


def kernel_sum(points, point_sq, sharpness, center_block, coef_block):
    products = lax.dot_general(
        points, center_block, (((1,), (1,)), ((), ())), preferred_element_type=jnp.float32
    )
    center_sq = jnp.sum(jnp.square(center_block.astype(jnp.float32)), axis=1)
    kernel = jnp.exp(-sharpness * (point_sq[:, None] + center_sq[None, :] - 2.0 * products)).astype(
        jnp.bfloat16
    )
    return jnp.dot(kernel, coef_block, preferred_element_type=jnp.float32)


def per_device(points, centers, coefficients, targets):
    features = points.shape[1]
    sharpness = 0.15 / math.sqrt(features)
    point_sq = jnp.sum(jnp.square(points.astype(jnp.float32)), axis=1)
    start_sum = jnp.zeros((points.shape[0], coefficients.shape[1]), jnp.float32)
    center_piece = lax.all_gather(centers, "blk", axis=0, tiled=True)
    coef_piece = lax.all_gather(coefficients, "blk", axis=0, tiled=True)
    piece_rows = center_piece.shape[0]
    block_rows = math.gcd(piece_rows, 256)
    block_count = piece_rows // block_rows
    center_blocks = center_piece.reshape(block_count, block_rows, features)
    coef_blocks = coef_piece.reshape(block_count, block_rows, coef_piece.shape[1])

    def step(inner_sum, blocks):
        return (inner_sum + kernel_sum(points, point_sq, sharpness, blocks[0], blocks[1]), None)

    result, _ = lax.scan(step, start_sum, (center_blocks, coef_blocks))
    predicted = lax.psum_scatter(result, "sum", scatter_dimension=1, tiled=True)
    return targets - predicted


def solution(mesh):
    return jax.shard_map(
        per_device,
        mesh=mesh,
        in_specs=(
            P(("grp", "blk"), None),
            P(("blk", "sum"), None),
            P(("blk", "sum"), None),
            P(("grp", "blk"), "sum"),
        ),
        out_specs=P(("grp", "blk"), "sum"),
        check_vma=False,
    )
```

profile of v0, /device:TPU:1, one launch (start us, length us, event | category | flops | bytes accessed | tf_op | source)
XLA Modules:
  0.0 91.3 jit_solution(9340841907587885446)
XLA Ops:
  6.5 0.0 copy-start
  6.5 0.0 all-gather.2.cloned.1.call-start
  6.5 0.7 all-gather.2.cloned.1.call-update
  7.3 0.0 reduce-scatter.2.cloned.1.call-start
  7.3 27.3 %all_gather.7 = bf16[1024,256]{1,0:T(8,128)(2,1)S(1)} all-gather(bf16[128,256]{1,0:T(8,128)(2,1)} %param.8), channel_id=1, replica_groups=mesh['grp'=2,'blk'=8,'sum'=2] {'blk'}, dimensions={0}, use_global_device_ids=true | all-gather | bytes 589824 | tf_op jit(solution)/shard_map/all_gather | solution.py:26
  34.6 2.1 %multiply_reduce_fusion.1 = f32[2048]{0:T(1024)S(1)} fusion(bf16[2048,512]{1,0:T(8,128)(2,1)} %param.6), kind=kLoop, calls=%fused_computation.19 | loop fusion | flops 3143680 | bytes 2105344 | tf_op jit(solution)/shard_map/reduce_sum | solution.py:23
  36.7 14.6 %all-gather.2.cloned.1.call-done = bf16[1024,512]{1,0:T(8,128)(2,1)} async-done(((bf16[128,512]{1,0:T(8,128)(2,1)}), bf16[1024,512]{1,0:T(8,128)(2,1)}) %all-gather.2.cloned.1.call-update) | async-done | bytes 1048592 | tf_op jit(solution)/shard_map/all_gather | solution.py:25
  51.2 0.0 copy-done
  51.2 20.6 %while.11 = (s32[]{:T(128)}, f32[2048,256]{1,0:T(8,128)}, f32[2048]{0:T(1024)S(1)}, bf16[4,256,512]{2,1,0:T(8,128)(2,1)}, bf16[2048,512]{1,0:T(8,128)(2,1)S(1)},...) while((s32[]{:T(128)}, f32[2048,256]{1,0:T(8,128)}, f32[2048]{0:T(1024)S(1)}, ...), condition=%wide.region_3.4_spmd.clone, body=%wide.region_1.3_spmd.clone.sunk | while | flops 809369344 | bytes 6958179 | solution.py:36
  51.2 1.1 %multiply_reduce_fusion.3 = f32[256]{0:T(256)S(1)} fusion(bf16[4,256,512]{2,1,0:T(8,128)(2,1)} %get-tuple-element.127, s32[]{:T(128)} %get-tuple-element.116), kind=kLoop, calls=%fused_computation.11.clone.1 | loop fusion | flops 392960 | bytes 263172 | tf_op jit(solution)/shard_map/while/body/eval_jaxpr/reduce_sum | solution.py:13
  52.3 3.5 %convolution_add_fusion.2 = f32[2048,256]{1,0:T(8,128)} fusion(f32[2048,256]{1,0:T(8,128)} %get-tuple-element.117, bf16[2048,512]{1,0:T(8,128)(2,1)S(1)} %get-tuple-element.128, f32[256]{0:T(256)S(1)} %multiply_reduce_fusion.3, f32[2048]{0:T(1024)S(1)} %get-tuple-element.126, pred[]{:T(512)S(6)} %compare.3, ...), kind=kOutput, calls=%fused_computation.5.clone.1 | convolution fusion | flops 808976384 | bytes 6694913 | tf_op jit(solution)/shard_map/while/body/eval_jaxpr/dot_general | solution.py:17
  55.8 1.1 %multiply_reduce_fusion.3 = f32[256]{0:T(256)S(1)} fusion(bf16[4,256,512]{2,1,0:T(8,128)(2,1)} %get-tuple-element.127, s32[]{:T(128)} %get-tuple-element.116), kind=kLoop, calls=%fused_computation.11.clone.1 | loop fusion | flops 392960 | bytes 263172 | tf_op jit(solution)/shard_map/while/body/eval_jaxpr/reduce_sum | solution.py:13
  56.9 4.2 %convolution_add_fusion.2 = f32[2048,256]{1,0:T(8,128)} fusion(f32[2048,256]{1,0:T(8,128)} %get-tuple-element.117, bf16[2048,512]{1,0:T(8,128)(2,1)S(1)} %get-tuple-element.128, f32[256]{0:T(256)S(1)} %multiply_reduce_fusion.3, f32[2048]{0:T(1024)S(1)} %get-tuple-element.126, pred[]{:T(512)S(6)} %compare.3, ...), kind=kOutput, calls=%fused_computation.5.clone.1 | convolution fusion | flops 808976384 | bytes 6694913 | tf_op jit(solution)/shard_map/while/body/eval_jaxpr/dot_general | solution.py:17
  61.2 1.1 %multiply_reduce_fusion.3 = f32[256]{0:T(256)S(1)} fusion(bf16[4,256,512]{2,1,0:T(8,128)(2,1)} %get-tuple-element.127, s32[]{:T(128)} %get-tuple-element.116), kind=kLoop, calls=%fused_computation.11.clone.1 | loop fusion | flops 392960 | bytes 263172 | tf_op jit(solution)/shard_map/while/body/eval_jaxpr/reduce_sum | solution.py:13
  62.2 4.2 %convolution_add_fusion.2 = f32[2048,256]{1,0:T(8,128)} fusion(f32[2048,256]{1,0:T(8,128)} %get-tuple-element.117, bf16[2048,512]{1,0:T(8,128)(2,1)S(1)} %get-tuple-element.128, f32[256]{0:T(256)S(1)} %multiply_reduce_fusion.3, f32[2048]{0:T(1024)S(1)} %get-tuple-element.126, pred[]{:T(512)S(6)} %compare.3, ...), kind=kOutput, calls=%fused_computation.5.clone.1 | convolution fusion | flops 808976384 | bytes 6694913 | tf_op jit(solution)/shard_map/while/body/eval_jaxpr/dot_general | solution.py:17
  66.5 1.1 %multiply_reduce_fusion.3 = f32[256]{0:T(256)S(1)} fusion(bf16[4,256,512]{2,1,0:T(8,128)(2,1)} %get-tuple-element.127, s32[]{:T(128)} %get-tuple-element.116), kind=kLoop, calls=%fused_computation.11.clone.1 | loop fusion | flops 392960 | bytes 263172 | tf_op jit(solution)/shard_map/while/body/eval_jaxpr/reduce_sum | solution.py:13
  67.6 4.2 %convolution_add_fusion.2 = f32[2048,256]{1,0:T(8,128)} fusion(f32[2048,256]{1,0:T(8,128)} %get-tuple-element.117, bf16[2048,512]{1,0:T(8,128)(2,1)S(1)} %get-tuple-element.128, f32[256]{0:T(256)S(1)} %multiply_reduce_fusion.3, f32[2048]{0:T(1024)S(1)} %get-tuple-element.126, pred[]{:T(512)S(6)} %compare.3, ...), kind=kOutput, calls=%fused_computation.5.clone.1 | convolution fusion | flops 808976384 | bytes 6694913 | tf_op jit(solution)/shard_map/while/body/eval_jaxpr/dot_general | solution.py:17
  71.8 0.0 copy-start.1
  71.8 0.0 reduce-scatter.2.cloned.1.call-update
  71.8 10.3 %reduce-scatter.2.cloned.1.call-done = f32[2048,128]{1,0:T(8,128)} async-done(((f32[2048,256]{1,0:T(8,128)}), f32[2048,128]{1,0:T(8,128)}) %reduce-scatter.2.cloned.1.call-update) | async-done | bytes 1048592 | tf_op jit(solution)/shard_map/reduce_scatter | solution.py:37
  82.1 0.0 copy-done.1
  82.1 2.3 %sub.6 = f32[2048,128]{1,0:T(8,128)} subtract(f32[2048,128]{1,0:T(8,128)S(1)} %copy-done.1, f32[2048,128]{1,0:T(8,128)} %reduce-scatter.2.cloned.1.call-done) | non-fusion elementwise | flops 262144 | bytes 3145728 | tf_op jit(solution)/shard_map/sub | solution.py:38
  (1 shorter events, 0.0 us)
Async XLA Ops:
  6.5 44.7 %copy-start = (bf16[2048,512]{1,0:T(8,128)(2,1)S(1)}, bf16[2048,512]{1,0:T(8,128)(2,1)}, u32[]{:S(2)}) copy-start(bf16[2048,512]{1,0:T(8,128)(2,1)} %param.6) | copy-start | bytes 6291460
  6.5 44.7 %all-gather.2.cloned.1.call-start = ((), (), s32[]{:S(2)}) async-start(), calls=%async_computation.1 | async-start | bytes 1179648 | tf_op jit(solution)/shard_map/all_gather | solution.py:25
  7.3 74.9 %reduce-scatter.2.cloned.1.call-start = ((), (), s32[]{:S(2)}) async-start(), calls=%async_computation.2 | async-start | bytes 3145728 | tf_op jit(solution)/shard_map/reduce_scatter | solution.py:37
  71.8 10.3 %copy-start.1 = (f32[2048,128]{1,0:T(8,128)S(1)}, f32[2048,128]{1,0:T(8,128)}, u32[]{:S(2)}) copy-start(f32[2048,128]{1,0:T(8,128)} %param.9) | copy-start | bytes 3145732
Sparse Core Ops, SparseCore 0:
  9.5 41.6 all-gather.1
  72.0 10.1 reduce-scatter.1
where the time goes:
time: 91.9 us; the launch traced here: 91.3 us
  blocking collectives  27.3 us (30%)
  waiting for transfers between devices  25.6 us (28%)
  matrix products  16.2 us (18%)
  between operations  13.4 us (15%)
  other arithmetic  8.69 us (9%)
    all_gather x1, blocking collectives, per_device(): coef_piece = lax.all_gather(coefficients, 'blk', axis=0, tiled=True)  27.3 us
    dot_general x4, matrix products, kernel_sum(): return jnp.dot(kernel, coef_block, preferred_element_type=jnp.float32)  16.2 us
    all_gather x1, waiting for transfers between devices, per_device(): center_piece = lax.all_gather(centers, 'blk', axis=0, tiled=True)  14.6 us
    reduce_scatter x1, waiting for transfers between devices, per_device(): predicted = lax.psum_scatter(result, 'sum', scatter_dimension=1, tiled=True)  10.3 us
    reduce_sum x4, other arithmetic, kernel_sum(): center_sq = jnp.sum(jnp.square(center_block.astype(jnp.float32)), axis=1)  4.32 us
    sub x1, other arithmetic, per_device(): return targets - predicted  2.3 us
    reduce_sum x1, other arithmetic, per_device(): point_sq = jnp.sum(jnp.square(points.astype(jnp.float32)), axis=1)  2.07 us
  transfers between devices with their start and end apart: 2, of which 2 were waited for; matrix products, arithmetic and copies ran while one was open for 2% of the time, Pallas kernels for 0%

commit v1 on v0

v1 whole, which is shorter than its diff:
```python
import functools
import math

import jax
import jax.numpy as jnp
from jax import lax
from jax.experimental import pallas as pl
from jax.experimental.pallas import tpu as pltpu
from jax.sharding import PartitionSpec as P

MESH = pl.DeviceIdType.MESH
TILE = 512
CHUNKS = 4


def ring_position(index, n):
    return jnp.where(lax.rem(index, 2) == 0, index // 2, n - 1 - index // 2) if n <= 8 else index


def ring_index(position, n):
    return jnp.where(position < n // 2, 2 * position, 2 * (n - 1 - position) + 1) if n <= 8 else position


def body(n, cross, points_hbm, centers_hbm, coef_hbm, out_ref,
         points, held, point_term, total, landed,
         local_sem, ring_send, ring_recv, x_send, x_recv, swap_send, swap_recv):
    rows, features = points.shape
    block = held.shape[1]
    columns = total.shape[2]
    half = n // 2
    me = ring_position(lax.axis_index("blk"), n)
    right = ring_index(lax.rem(me + 1, n), n)
    left = ring_index(lax.rem(me + n - 1, n), n)
    mine = lax.axis_index("sum")
    other = 1 - mine
    group = lax.axis_index("grp")
    side = lax.rem(group, 2)
    sharpness = 0.15 / math.sqrt(features)
    scale = -sharpness * math.log2(math.e)

    copies = [
        pltpu.make_async_copy(centers_hbm, held.at[0, :, pl.ds(0, features)], local_sem.at[0]),
        pltpu.make_async_copy(coef_hbm, held.at[0, :, pl.ds(features, 2 * columns)], local_sem.at[1]),
        pltpu.make_async_copy(points_hbm, points, local_sem.at[2]),
    ]
    for copy in copies:
        copy.start()

    barrier = pltpu.get_barrier_semaphore()
    greet = [{"blk": left}, {"blk": right}, {"sum": other}]
    partner = {"grp": group + 1 - 2 * side}
    if cross:
        greet.append(partner)
    for device in greet:
        pl.semaphore_signal(barrier, inc=1, device_id=device, device_id_type=MESH)
    pl.semaphore_wait(barrier, len(greet))

    only = (3 * block // 8) // 16 * 16
    both = block - 2 * only
    if cross:
        parts = (pl.ds(pl.multiple_of(side * (only + both), 16), only), pl.ds(only, both))
    else:
        parts = (pl.ds(0, block // 2), pl.ds(block // 2, block // 2))

    def slot(way, d):
        if d == 0:
            return 0
        return n - 1 if d == half else 2 * d - 1 + way

    ring = {}
    for d in range(1, half + 1):
        for way in (0, 1):
            for part in (0, 1):
                if d == half and part != way:
                    continue
                ring[way, d, part] = pltpu.make_async_remote_copy(
                    src_ref=held.at[slot(way, d - 1), parts[part]],
                    dst_ref=held.at[slot(way, d), parts[part]],
                    send_sem=ring_send.at[way, d - 1, part],
                    recv_sem=ring_recv.at[way, d - 1, part],
                    device_id={"blk": (right, left)[way]},
                    device_id_type=MESH,
                )
    over = {}
    if cross:
        for s in range(1, n):
            over[s] = pltpu.make_async_remote_copy(
                src_ref=held.at[s, parts[0]], dst_ref=held.at[s, parts[0]],
                send_sem=x_send.at[s], recv_sem=x_recv.at[s],
                device_id=partner, device_id_type=MESH,
            )

    def row_sums(a, b):
        return lax.dot_general(a, b, (((1,), (1,)), ((), ())), preferred_element_type=jnp.float32)

    def split_square(v):
        square = jnp.square(v.astype(jnp.float32))
        high = square.astype(jnp.bfloat16)
        return high, (square - high.astype(jnp.float32)).astype(jnp.bfloat16)

    def prepare(first, count):
        size = count * block
        c = held[first:first + count, :, 0:features].reshape(size, features)
        w = held[first:first + count, :, features:features + 2 * columns].reshape(size, 2 * columns)
        high, low = split_square(c)
        ones = jnp.ones((16, features), jnp.bfloat16)
        term = scale * (row_sums(ones, high) + row_sums(ones, low))[0:1, :]
        return c, w, term

    def tile_sum(c, w, term, at, tile):
        products = row_sums(points[pl.ds(at, tile), :], c)
        a = point_term[pl.ds(at, tile), :]
        pieces = []
        for lane in range(0, c.shape[0], 128):
            exponent = (a + term[:, lane:lane + 128]) - (2.0 * scale) * products[:, lane:lane + 128]
            pieces.append(jnp.exp2(exponent).astype(jnp.bfloat16))
        kernel = pieces[0] if len(pieces) == 1 else jnp.concatenate(pieces, axis=1)
        return jnp.dot(kernel, w, preferred_element_type=jnp.float32)

    def group_sum(first, count, fresh):
        c, w, term = prepare(first, count)

        @pl.loop(0, rows // TILE)
        def _(i):
            at = pl.multiple_of(i * TILE, TILE)
            got = tile_sum(c, w, term, at, TILE)
            for h in (0, 1):
                piece = got[:, h * columns:(h + 1) * columns]
                if fresh:
                    total[h, pl.ds(at, TILE), :] = piece
                else:
                    total[h, pl.ds(at, TILE), :] += piece

    copies[0].wait()
    copies[1].wait()
    for part in (0, 1):
        for way in (0, 1):
            if (way, 1, part) in ring:
                ring[way, 1, part].start()

    copies[2].wait()

    @pl.loop(0, rows // TILE)
    def _(i):
        at = pl.multiple_of(i * TILE, TILE)
        high, low = split_square(points[pl.ds(at, TILE), :])
        ones = jnp.ones((128, features), jnp.bfloat16)
        point_term[pl.ds(at, TILE), :] = scale * (row_sums(high, ones) + row_sums(low, ones))

    group_sum(0, 1, True)
    for d in range(1, half + 1):
        for part in (0, 1):
            for way in (0, 1):
                if (way, d, part) not in ring:
                    continue
                ring[way, d, part].wait_recv()
                if (way, d + 1, part) in ring:
                    ring[way, d + 1, part].start()
                if cross and part == 0:
                    over[slot(way, d)].start()
        if d > 1:
            if cross:
                over[slot(0, d - 1)].wait_recv()
                over[slot(1, d - 1)].wait_recv()
            group_sum(slot(0, d - 1), 2, False)

    if cross:
        over[n - 1].wait_recv()
    c, w, term = prepare(n - 1, 1)
    size = rows // CHUNKS
    swaps = []
    for i in range(CHUNKS):
        got = tile_sum(c, w, term, i * size, size)
        for h in (0, 1):
            total[h, i * size:(i + 1) * size, :] += got[:, h * columns:(h + 1) * columns]
        swap = pltpu.make_async_remote_copy(
            src_ref=total.at[other, pl.ds(i * size, size)],
            dst_ref=landed.at[pl.ds(i * size, size)],
            send_sem=swap_send.at[i], recv_sem=swap_recv.at[i],
            device_id={"sum": other}, device_id_type=MESH,
        )
        swap.start()
        swaps.append(swap)
    for i in range(CHUNKS):
        swaps[i].wait_recv()
        at = pl.ds(i * size, size)
        out_ref[at, :] = total[mine, at, :] + landed[at, :]
    for copy in (*ring.values(), *over.values(), *swaps):
        copy.wait_send()


def per_device(n, cross, points, centers, coefficients, targets):
    rows, features = points.shape
    block = centers.shape[0]
    width = coefficients.shape[1]
    columns = targets.shape[1]
    half = n // 2
    predicted = pl.pallas_call(
        functools.partial(body, n, cross),
        out_shape=jax.ShapeDtypeStruct((rows, columns), jnp.float32),
        in_specs=[pl.BlockSpec(memory_space=pltpu.HBM)] * 3,
        out_specs=pl.BlockSpec(memory_space=pltpu.VMEM),
        scratch_shapes=[
            pltpu.VMEM((rows, features), jnp.bfloat16),
            pltpu.VMEM((n, block, features + width), jnp.bfloat16),
            pltpu.VMEM((rows, 128), jnp.float32),
            pltpu.VMEM((2, rows, columns), jnp.float32),
            pltpu.VMEM((rows, columns), jnp.float32),
            pltpu.SemaphoreType.DMA((3,)),
            pltpu.SemaphoreType.DMA((2, half, 2)),
            pltpu.SemaphoreType.DMA((2, half, 2)),
            pltpu.SemaphoreType.DMA((n,)),
            pltpu.SemaphoreType.DMA((n,)),
            pltpu.SemaphoreType.DMA((CHUNKS,)),
            pltpu.SemaphoreType.DMA((CHUNKS,)),
        ],
        compiler_params=pltpu.CompilerParams(
            collective_id=0, has_side_effects=True, vmem_limit_bytes=40 * 2**20
        ),
        cost_estimate=pl.CostEstimate(
            flops=2 * rows * n * block * (features + width),
            bytes_accessed=2 * rows * features + 4 * rows * columns,
            transcendentals=rows * n * block,
        ),
    )(points, centers, coefficients)
    return targets - predicted


def solution(mesh):
    return jax.shard_map(
        functools.partial(per_device, mesh.shape["blk"], mesh.shape["grp"] % 2 == 0),
        mesh=mesh,
        in_specs=(
            P(("grp", "blk"), None),
            P(("blk", "sum"), None),
            P(("blk", "sum"), None),
            P(("grp", "blk"), "sum"),
        ),
        out_specs=P(("grp", "blk"), "sum"),
        check_vma=False,
    )
```

time: 91.9 us -> 31.2 us (0.34)
  blocking collectives: 27.3 us -> 0 us
  Pallas kernels: 0 us -> 26.6 us
  waiting for transfers between devices: 25.6 us -> 0 us
  matrix products: 16.2 us -> 0 us
  between operations: 13.4 us -> 0.02 us
  other arithmetic: 8.69 us -> 1.08 us
  local copies, waits for them, and re-layouts: 0.01 us -> 3.34 us
    all_gather x1 -> x0, blocking collectives: 27.3 us -> none  [per_device(): coef_piece = lax.all_gather(coefficients, 'blk', axis=0, tiled=True)]
    pallas_call x0 -> x1, Pallas kernels: none -> 26.6 us  [per_device(): pl.pallas_call(functools.partial(body, n, cross), out_shape=jax.ShapeDtyp...]
    dot_general x4 -> x0, matrix products: 16.2 us -> none  [kernel_sum(): return jnp.dot(kernel, coef_block, preferred_element_type=jnp.float32)]
    all_gather x1 -> x0, waiting for transfers between devices: 14.6 us -> none  [per_device(): center_piece = lax.all_gather(centers, 'blk', axis=0, tiled=True)]
    reduce_scatter x1 -> x0, waiting for transfers between devices: 10.3 us -> none  [per_device(): predicted = lax.psum_scatter(result, 'sum', scatter_dimension=1, tiled=True)]
    reduce_sum x5 -> x0, other arithmetic: 6.39 us -> none  [the longest x4 4.32 us: kernel_sum(): center_sq = jnp.sum(jnp.square(center_block.astype(jnp.float32)), axis=1)]
    unnamed x4 -> x8, local copies, waits for them, and re-layouts: 0.01 us -> 3.34 us
    sub x1, other arithmetic: 2.3 us -> 1.08 us  [per_device(): return targets - predicted]
  transfers between devices with their start and end apart: 2 -> 0, of which waited for: 2 -> 0; matrix products, arithmetic and copies ran while one was open for 2% -> 0% of each run, Pallas kernels for 0% -> 0%
where the time goes in v1:
time: 31.2 us; the launch traced here: 31 us
  Pallas kernels  26.6 us (85%)
  local copies, waits for them, and re-layouts  3.34 us (11%)
  other arithmetic  1.08 us (3%)
    pallas_call x1, Pallas kernels, per_device(): pl.pallas_call(functools.partial(body, n, cross), out_shape=jax.ShapeDtyp...  26.6 us
    unnamed x8, local copies, waits for them, and re-layouts  3.34 us
    sub x1, other arithmetic, per_device(): return targets - predicted  1.08 us

profile of v1, /device:TPU:1, one launch (start us, length us, event | category | flops | bytes accessed | tf_op | source)
XLA Modules:
  0.0 31.0 jit_solution(16620562332464479074)
XLA Ops:
  0.0 0.0 copy-start
  0.0 1.6 %copy-done = bf16[2048,512]{1,0:T(8,128)(2,1)S(1)} copy-done((bf16[2048,512]{1,0:T(8,128)(2,1)S(1)}, bf16[2048,512]{1,0:T(8,128)(2,1)}, u32[]{:S(2)}) %copy-start) | copy-done | bytes 2097176
  1.6 0.0 copy-start.1
  1.6 0.9 %copy-done.1 = bf16[128,512]{1,0:T(8,128)(2,1)S(1)} copy-done((bf16[128,512]{1,0:T(8,128)(2,1)S(1)}, bf16[128,512]{1,0:T(8,128)(2,1)}, u32[]{:S(2)}) %copy-start.1) | copy-done | bytes 131096
  2.5 0.0 copy-start.2
  2.5 0.8 %copy-done.2 = bf16[128,256]{1,0:T(8,128)(2,1)S(1)} copy-done((bf16[128,256]{1,0:T(8,128)(2,1)S(1)}, bf16[128,256]{1,0:T(8,128)(2,1)}, u32[]{:S(2)}) %copy-start.2) | copy-done | bytes 65560
  3.3 0.0 copy-start.3
  3.3 26.6 %shard_map.46 = f32[2048,128]{1,0:T(8,128)S(1)} custom-call(bf16[2048,512]{1,0:T(8,128)(2,1)S(1)} %copy-done, bf16[128,512]{1,0:T(8,128)(2,1)S(1)} %copy-done.1, bf16[128,256]{1,0:T(8,128)(2,1)S(1)} %copy-done.2), custom_call_target="tpu_custom_call" | custom-call | flops 3221225472 | bytes 3145728 | tf_op jit(solution)/shard_map/pallas_call | solution.py:198
  29.9 0.0 copy-done.3
  29.9 1.1 %sub.3 = f32[2048,128]{1,0:T(8,128)} subtract(f32[2048,128]{1,0:T(8,128)S(1)} %copy-done.3, f32[2048,128]{1,0:T(8,128)S(1)} %shard_map.46) | non-fusion elementwise | flops 262144 | bytes 3145728 | tf_op jit(solution)/shard_map/sub | solution.py:226
Async XLA Ops:
  0.0 1.6 %copy-start = (bf16[2048,512]{1,0:T(8,128)(2,1)S(1)}, bf16[2048,512]{1,0:T(8,128)(2,1)}, u32[]{:S(2)}) copy-start(bf16[2048,512]{1,0:T(8,128)(2,1)} %points_hbm.1) | copy-start | bytes 6291460
  1.6 0.9 %copy-start.1 = (bf16[128,512]{1,0:T(8,128)(2,1)S(1)}, bf16[128,512]{1,0:T(8,128)(2,1)}, u32[]{:S(2)}) copy-start(bf16[128,512]{1,0:T(8,128)(2,1)} %centers_hbm.1) | copy-start | bytes 393220
  2.5 0.8 %copy-start.2 = (bf16[128,256]{1,0:T(8,128)(2,1)S(1)}, bf16[128,256]{1,0:T(8,128)(2,1)}, u32[]{:S(2)}) copy-start(bf16[128,256]{1,0:T(8,128)(2,1)} %coef_hbm.1) | copy-start | bytes 196612
  3.3 26.6 %copy-start.3 = (f32[2048,128]{1,0:T(8,128)S(1)}, f32[2048,128]{1,0:T(8,128)}, u32[]{:S(2)}) copy-start(f32[2048,128]{1,0:T(8,128)} %param.7) | copy-start | bytes 3145732

commit v2 on v1

--- a/solution.py
+++ b/solution.py
@@ -11,6 +11,8 @@
 MESH = pl.DeviceIdType.MESH
 TILE = 512
 CHUNKS = 4
+PIECES = ((16, 32), (32,))
+FIRST = 2
 
 
 def ring_position(index, n):
@@ -55,12 +57,20 @@
         pl.semaphore_signal(barrier, inc=1, device_id=device, device_id_type=MESH)
     pl.semaphore_wait(barrier, len(greet))
 
-    only = (3 * block // 8) // 16 * 16
-    both = block - 2 * only
-    if cross:
-        parts = (pl.ds(pl.multiple_of(side * (only + both), 16), only), pl.ds(only, both))
-    else:
-        parts = (pl.ds(0, block // 2), pl.ds(block // 2, block // 2))
+    pieces = []
+    start = 0
+    only = sum(PIECES[0]) * block // 128
+    base = side * (block - only) if cross else 0
+    for size in (size * block // 128 for size in PIECES[0]):
+        pieces.append((pl.ds(pl.multiple_of(base + start, 16), size), True))
+        start += size
+    start, end = only, block - only if cross else block
+    sizes = [size * block // 128 for size in PIECES[1]]
+    sizes[-1] = end - start - sum(sizes[:-1])
+    for size in sizes:
+        pieces.append((pl.ds(start, size), False))
+        start += size
+    count = len(pieces)
 
     def slot(way, d):
         if d == 0:
@@ -70,12 +80,12 @@
     ring = {}
     for d in range(1, half + 1):
         for way in (0, 1):
-            for part in (0, 1):
-                if d == half and part != way:
+            for part in range(count):
+                if d == half and way != (part >= FIRST):
                     continue
                 ring[way, d, part] = pltpu.make_async_remote_copy(
-                    src_ref=held.at[slot(way, d - 1), parts[part]],
-                    dst_ref=held.at[slot(way, d), parts[part]],
+                    src_ref=held.at[slot(way, d - 1), pieces[part][0]],
+                    dst_ref=held.at[slot(way, d), pieces[part][0]],
                     send_sem=ring_send.at[way, d - 1, part],
                     recv_sem=ring_recv.at[way, d - 1, part],
                     device_id={"blk": (right, left)[way]},
@@ -84,11 +94,12 @@
     over = {}
     if cross:
         for s in range(1, n):
-            over[s] = pltpu.make_async_remote_copy(
-                src_ref=held.at[s, parts[0]], dst_ref=held.at[s, parts[0]],
-                send_sem=x_send.at[s], recv_sem=x_recv.at[s],
-                device_id=partner, device_id_type=MESH,
-            )
+            for part in range(len(PIECES[0])):
+                over[s, part] = pltpu.make_async_remote_copy(
+                    src_ref=held.at[s, pieces[part][0]], dst_ref=held.at[s, pieces[part][0]],
+                    send_sem=x_send.at[s, part], recv_sem=x_recv.at[s, part],
+                    device_id=partner, device_id_type=MESH,
+                )
 
     def row_sums(a, b):
         return lax.dot_general(a, b, (((1,), (1,)), ((), ())), preferred_element_type=jnp.float32)
@@ -110,11 +121,11 @@
     def tile_sum(c, w, term, at, tile):
         products = row_sums(points[pl.ds(at, tile), :], c)
         a = point_term[pl.ds(at, tile), :]
-        pieces = []
+        parts = []
         for lane in range(0, c.shape[0], 128):
             exponent = (a + term[:, lane:lane + 128]) - (2.0 * scale) * products[:, lane:lane + 128]
-            pieces.append(jnp.exp2(exponent).astype(jnp.bfloat16))
-        kernel = pieces[0] if len(pieces) == 1 else jnp.concatenate(pieces, axis=1)
+            parts.append(jnp.exp2(exponent).astype(jnp.bfloat16))
+        kernel = parts[0] if len(parts) == 1 else jnp.concatenate(parts, axis=1)
         return jnp.dot(kernel, w, preferred_element_type=jnp.float32)
 
     def group_sum(first, count, fresh):
@@ -133,7 +144,7 @@
 
     copies[0].wait()
     copies[1].wait()
-    for part in (0, 1):
+    for part in range(count):
         for way in (0, 1):
             if (way, 1, part) in ring:
                 ring[way, 1, part].start()
@@ -149,23 +160,25 @@
 
     group_sum(0, 1, True)
     for d in range(1, half + 1):
-        for part in (0, 1):
+        for part in range(count):
             for way in (0, 1):
                 if (way, d, part) not in ring:
                     continue
                 ring[way, d, part].wait_recv()
                 if (way, d + 1, part) in ring:
                     ring[way, d + 1, part].start()
-                if cross and part == 0:
-                    over[slot(way, d)].start()
+                if cross and pieces[part][1]:
+                    over[slot(way, d), part].start()
         if d > 1:
             if cross:
-                over[slot(0, d - 1)].wait_recv()
-                over[slot(1, d - 1)].wait_recv()
+                for part in range(len(PIECES[0])):
+                    over[slot(0, d - 1), part].wait_recv()
+                    over[slot(1, d - 1), part].wait_recv()
             group_sum(slot(0, d - 1), 2, False)
 
     if cross:
-        over[n - 1].wait_recv()
+        for part in range(len(PIECES[0])):
+            over[n - 1, part].wait_recv()
     c, w, term = prepare(n - 1, 1)
     size = rows // CHUNKS
     swaps = []
@@ -198,7 +211,7 @@
     predicted = pl.pallas_call(
         functools.partial(body, n, cross),
         out_shape=jax.ShapeDtypeStruct((rows, columns), jnp.float32),
-        in_specs=[pl.BlockSpec(memory_space=pltpu.HBM)] * 3,
+        in_specs=[pl.BlockSpec(memory_space=pl.ANY)] * 3,
         out_specs=pl.BlockSpec(memory_space=pltpu.VMEM),
         scratch_shapes=[
             pltpu.VMEM((rows, features), jnp.bfloat16),
@@ -207,15 +220,15 @@
             pltpu.VMEM((2, rows, columns), jnp.float32),
             pltpu.VMEM((rows, columns), jnp.float32),
             pltpu.SemaphoreType.DMA((3,)),
-            pltpu.SemaphoreType.DMA((2, half, 2)),
-            pltpu.SemaphoreType.DMA((2, half, 2)),
-            pltpu.SemaphoreType.DMA((n,)),
-            pltpu.SemaphoreType.DMA((n,)),
+            pltpu.SemaphoreType.DMA((2, half, len(PIECES[0]) + len(PIECES[1]))),
+            pltpu.SemaphoreType.DMA((2, half, len(PIECES[0]) + len(PIECES[1]))),
+            pltpu.SemaphoreType.DMA((n, len(PIECES[0]))),
+            pltpu.SemaphoreType.DMA((n, len(PIECES[0]))),
             pltpu.SemaphoreType.DMA((CHUNKS,)),
             pltpu.SemaphoreType.DMA((CHUNKS,)),
         ],
         compiler_params=pltpu.CompilerParams(
-            collective_id=0, has_side_effects=True, vmem_limit_bytes=40 * 2**20
+            collective_id=0, has_side_effects=True, vmem_limit_bytes=60 * 2**20
         ),
         cost_estimate=pl.CostEstimate(
             flops=2 * rows * n * block * (features + width),

time: 31.2 us -> 29.8 us (0.955)
  local copies, waits for them, and re-layouts: 3.34 us -> 0.01 us
  other arithmetic: 1.08 us -> 2.3 us
  Pallas kernels: 26.6 us -> 27.4 us
    unnamed x8 -> x2, local copies, waits for them, and re-layouts: 3.34 us -> 0.01 us
    sub x1, other arithmetic: 1.08 us -> 2.3 us  [per_device(): return targets - predicted]
    pallas_call x1, Pallas kernels: 26.6 us -> 27.4 us  [per_device(): pl.pallas_call(functools.partial(body, n, cross), out_shape=jax.ShapeDtyp...]
where the time goes in v2:
time: 29.8 us; the launch traced here: 29.7 us
  Pallas kernels  27.4 us (92%)
  other arithmetic  2.3 us (8%)
    pallas_call x1, Pallas kernels, per_device(): pl.pallas_call(functools.partial(body, n, cross), out_shape=jax.ShapeDtyp...  27.4 us
    sub x1, other arithmetic, per_device(): return targets - predicted  2.3 us

profile of v2, /device:TPU:1, one launch (start us, length us, event | category | flops | bytes accessed | tf_op | source)
XLA Modules:
  0.0 29.7 jit_solution(1120836352630975508)
XLA Ops:
  0.0 0.0 copy-start
  0.0 27.4 %shard_map.46 = f32[2048,128]{1,0:T(8,128)} custom-call(bf16[2048,512]{1,0:T(8,128)(2,1)} %points_hbm.1, bf16[128,512]{1,0:T(8,128)(2,1)} %centers_hbm.1, bf16[128,256]{1,0:T(8,128)(2,1)} %coef_hbm.1), custom_call_target="tpu_custom_call" | custom-call | flops 3221225472 | bytes 3145728 | tf_op jit(solution)/shard_map/pallas_call | solution.py:211
  27.4 0.0 copy-done
  27.4 2.3 %sub.3 = f32[2048,128]{1,0:T(8,128)} subtract(f32[2048,128]{1,0:T(8,128)S(1)} %copy-done, f32[2048,128]{1,0:T(8,128)} %shard_map.46) | non-fusion elementwise | flops 262144 | bytes 3145728 | tf_op jit(solution)/shard_map/sub | solution.py:239
Async XLA Ops:
  0.0 27.4 %copy-start = (f32[2048,128]{1,0:T(8,128)S(1)}, f32[2048,128]{1,0:T(8,128)}, u32[]{:S(2)}) copy-start(f32[2048,128]{1,0:T(8,128)} %param.7) | copy-start | bytes 3145732

commit v3 on v2

--- a/solution.py
+++ b/solution.py
@@ -210,7 +210,7 @@
     half = n // 2
     predicted = pl.pallas_call(
         functools.partial(body, n, cross),
-        out_shape=jax.ShapeDtypeStruct((rows, columns), jnp.float32),
+        out_shape=pltpu.VMEM((rows, columns), jnp.float32),
         in_specs=[pl.BlockSpec(memory_space=pl.ANY)] * 3,
         out_specs=pl.BlockSpec(memory_space=pltpu.VMEM),
         scratch_shapes=[
@@ -228,7 +228,7 @@
             pltpu.SemaphoreType.DMA((CHUNKS,)),
         ],
         compiler_params=pltpu.CompilerParams(
-            collective_id=0, has_side_effects=True, vmem_limit_bytes=60 * 2**20
+            collective_id=0, has_side_effects=True, vmem_limit_bytes=58 * 2**20
         ),
         cost_estimate=pl.CostEstimate(
             flops=2 * rows * n * block * (features + width),

time: 29.8 us -> 27.6 us (0.926)
  other arithmetic: 2.3 us -> 1.08 us
  Pallas kernels: 27.4 us -> 26.4 us
    sub x1, other arithmetic: 2.3 us -> 1.08 us  [per_device(): return targets - predicted]
    pallas_call x1, Pallas kernels: 27.4 us -> 26.4 us  [per_device(): pl.pallas_call(functools.partial(body, n, cross), out_shape=pltpu.VMEM((r...]
where the time goes in v3:
time: 27.6 us; the launch traced here: 27.5 us
  Pallas kernels  26.4 us (96%)
  other arithmetic  1.08 us (4%)
    pallas_call x1, Pallas kernels, per_device(): pl.pallas_call(functools.partial(body, n, cross), out_shape=pltpu.VMEM((r...  26.4 us
    sub x1, other arithmetic, per_device(): return targets - predicted  1.08 us

profile of v3, /device:TPU:1, one launch (start us, length us, event | category | flops | bytes accessed | tf_op | source)
XLA Modules:
  0.0 27.5 jit_solution(2751116294160292165)
XLA Ops:
  0.0 0.0 copy-start
  0.0 26.4 %shard_map.46 = f32[2048,128]{1,0:T(8,128)S(1)} custom-call(bf16[2048,512]{1,0:T(8,128)(2,1)} %points_hbm.1, bf16[128,512]{1,0:T(8,128)(2,1)} %centers_hbm.1, bf16[128,256]{1,0:T(8,128)(2,1)} %coef_hbm.1), custom_call_target="tpu_custom_call" | custom-call | flops 3221225472 | bytes 3145728 | tf_op jit(solution)/shard_map/pallas_call | solution.py:211
  26.4 0.0 copy-done
  26.4 1.1 %sub.3 = f32[2048,128]{1,0:T(8,128)} subtract(f32[2048,128]{1,0:T(8,128)S(1)} %copy-done, f32[2048,128]{1,0:T(8,128)S(1)} %shard_map.46) | non-fusion elementwise | flops 262144 | bytes 3145728 | tf_op jit(solution)/shard_map/sub | solution.py:239
Async XLA Ops:
  0.0 26.4 %copy-start = (f32[2048,128]{1,0:T(8,128)S(1)}, f32[2048,128]{1,0:T(8,128)}, u32[]{:S(2)}) copy-start(f32[2048,128]{1,0:T(8,128)} %param.7) | copy-start | bytes 3145732

commit v4 on v3

--- a/solution.py
+++ b/solution.py
@@ -9,7 +9,7 @@
 from jax.sharding import PartitionSpec as P
 
 MESH = pl.DeviceIdType.MESH
-TILE = 512
+TILE = 1024
 CHUNKS = 4
 PIECES = ((16, 32), (32,))
 FIRST = 2
@@ -158,7 +158,6 @@
         ones = jnp.ones((128, features), jnp.bfloat16)
         point_term[pl.ds(at, TILE), :] = scale * (row_sums(high, ones) + row_sums(low, ones))
 
-    group_sum(0, 1, True)
     for d in range(1, half + 1):
         for part in range(count):
             for way in (0, 1):
@@ -169,7 +168,9 @@
                     ring[way, d + 1, part].start()
                 if cross and pieces[part][1]:
                     over[slot(way, d), part].start()
-        if d > 1:
+        if d == 1:
+            group_sum(0, 1, True)
+        else:
             if cross:
                 for part in range(len(PIECES[0])):
                     over[slot(0, d - 1), part].wait_recv()

time: 27.6 us -> 26.8 us (0.971)
  Pallas kernels: 26.4 us -> 25.6 us
    pallas_call x1, Pallas kernels: 26.4 us -> 25.6 us  [per_device(): pl.pallas_call(functools.partial(body, n, cross), out_shape=pltpu.VMEM((r...]
where the time goes in v4:
time: 26.8 us; the launch traced here: 26.7 us
  Pallas kernels  25.6 us (96%)
  other arithmetic  1.08 us (4%)
    pallas_call x1, Pallas kernels, per_device(): pl.pallas_call(functools.partial(body, n, cross), out_shape=pltpu.VMEM((r...  25.6 us
    sub x1, other arithmetic, per_device(): return targets - predicted  1.08 us

profile of v4, /device:TPU:1, one launch (start us, length us, event | category | flops | bytes accessed | tf_op | source)
XLA Modules:
  0.0 26.7 jit_solution(2644952117878117378)
XLA Ops:
  0.0 0.0 copy-start
  0.0 25.6 %shard_map.46 = f32[2048,128]{1,0:T(8,128)S(1)} custom-call(bf16[2048,512]{1,0:T(8,128)(2,1)} %points_hbm.1, bf16[128,512]{1,0:T(8,128)(2,1)} %centers_hbm.1, bf16[128,256]{1,0:T(8,128)(2,1)} %coef_hbm.1), custom_call_target="tpu_custom_call" | custom-call | flops 3221225472 | bytes 3145728 | tf_op jit(solution)/shard_map/pallas_call | solution.py:212
  25.6 0.0 copy-done
  25.6 1.1 %sub.3 = f32[2048,128]{1,0:T(8,128)} subtract(f32[2048,128]{1,0:T(8,128)S(1)} %copy-done, f32[2048,128]{1,0:T(8,128)S(1)} %shard_map.46) | non-fusion elementwise | flops 262144 | bytes 3145728 | tf_op jit(solution)/shard_map/sub | solution.py:240
Async XLA Ops:
  0.0 25.6 %copy-start = (f32[2048,128]{1,0:T(8,128)S(1)}, f32[2048,128]{1,0:T(8,128)}, u32[]{:S(2)}) copy-start(f32[2048,128]{1,0:T(8,128)} %param.7) | copy-start | bytes 3145732

commit v5 on v4

--- a/solution.py
+++ b/solution.py
@@ -9,7 +9,7 @@
 from jax.sharding import PartitionSpec as P
 
 MESH = pl.DeviceIdType.MESH
-TILE = 1024
+TILE = 2048
 CHUNKS = 4
 PIECES = ((16, 32), (32,))
 FIRST = 2

time: 26.8 us -> 26.5 us (0.989)
  Pallas kernels: 25.6 us -> 25.3 us
    pallas_call x1, Pallas kernels: 25.6 us -> 25.3 us  [per_device(): pl.pallas_call(functools.partial(body, n, cross), out_shape=pltpu.VMEM((r...]
where the time goes in v5:
time: 26.5 us; the launch traced here: 26.4 us
  Pallas kernels  25.3 us (95%)
  other arithmetic  1.08 us (4%)
    pallas_call x1, Pallas kernels, per_device(): pl.pallas_call(functools.partial(body, n, cross), out_shape=pltpu.VMEM((r...  25.3 us
    sub x1, other arithmetic, per_device(): return targets - predicted  1.08 us

profile of v5, /device:TPU:1, one launch (start us, length us, event | category | flops | bytes accessed | tf_op | source)
XLA Modules:
  0.0 26.4 jit_solution(14486444556320465537)
XLA Ops:
  0.0 0.0 copy-start
  0.0 25.3 %shard_map.46 = f32[2048,128]{1,0:T(8,128)S(1)} custom-call(bf16[2048,512]{1,0:T(8,128)(2,1)} %points_hbm.1, bf16[128,512]{1,0:T(8,128)(2,1)} %centers_hbm.1, bf16[128,256]{1,0:T(8,128)(2,1)} %coef_hbm.1), custom_call_target="tpu_custom_call" | custom-call | flops 3221225472 | bytes 3145728 | tf_op jit(solution)/shard_map/pallas_call | solution.py:212
  25.3 0.0 copy-done
  25.3 1.1 %sub.3 = f32[2048,128]{1,0:T(8,128)} subtract(f32[2048,128]{1,0:T(8,128)S(1)} %copy-done, f32[2048,128]{1,0:T(8,128)S(1)} %shard_map.46) | non-fusion elementwise | flops 262144 | bytes 3145728 | tf_op jit(solution)/shard_map/sub | solution.py:240
Async XLA Ops:
  0.0 25.3 %copy-start = (f32[2048,128]{1,0:T(8,128)S(1)}, f32[2048,128]{1,0:T(8,128)}, u32[]{:S(2)}) copy-start(f32[2048,128]{1,0:T(8,128)} %param.7) | copy-start | bytes 3145732
